TPU v7x, 32 devices: a whole 2x2x4 slice. The times are simulated.
32 devices in a mesh: docs: 8 (over z, core), protos: 4 (over y, x).
Axes of the slice: x: 2, y: 2, z: 4, core: 2. Of those that a mesh axis runs over, the one named last changes fastest.
Arguments:
- embeddings: bfloat16 [8192, 512], P('docs'), may hold values from -12.5 to 12.5
- prototypes: bfloat16 [65536, 512], P('protos'), may hold values from -4 to 4
Outputs:
- new_prototypes: bfloat16 [65536, 512], P(('protos', 'docs'))
- column_potential: float32 [65536], P('protos')
- row_potential: float32 [8192], P('docs')
All inputs are finite; a program needn't handle non-finite values.
Results may differ from a plain program's by a relative error of at most 0.0035.
Values may be sent and summed in bfloat16 or wider, within the bound.
No kernel may reach another device: no remote copies, remote signals or barrier semaphores. Data moves between devices by JAX's collectives and lax.ppermute only.
A program may use at most 256 MiB of HBM per device.

v0:
```python
import math
import jax
import jax.numpy as jnp
from jax import lax
from jax.sharding import PartitionSpec as P

SWEEPS = 2


def on_device(embeddings, prototypes):
    local_docs = embeddings.shape[0]
    local_protos = prototypes.shape[0]
    total_docs = local_docs * lax.axis_size("docs")
    total_protos = local_protos * lax.axis_size("protos")
    logit_gain = 4.0 / math.sqrt(embeddings.shape[1])
    scores = (
        lax.dot_general(
            embeddings, prototypes, (((1,), (1,)), ((), ())), preferred_element_type=jnp.float32
        )
        * logit_gain
    )
    row_peak = lax.pmax(jnp.max(scores, axis=1), "protos")
    numerators = jnp.exp(scores - row_peak[:, None])
    row_total = lax.psum(jnp.sum(numerators, axis=1), "protos")
    rescale = 1.0
    row_scale = 1.0 / row_total
    row_weight = rescale * row_scale
    col_scale = jnp.zeros((local_protos,), jnp.float32)
    for sweep_index in range(SWEEPS):
        col_local = jnp.dot(
            row_weight,
            numerators,
            precision=lax.Precision.HIGHEST,
            preferred_element_type=jnp.float32,
        )
        col_total = lax.psum(col_local, "docs")
        col_scale = 1.0 / (total_protos * col_total)
        row_local = rescale * jnp.dot(
            numerators,
            col_scale,
            precision=lax.Precision.HIGHEST,
            preferred_element_type=jnp.float32,
        )
        row_sum = lax.psum(row_local, "protos")
        row_scale = 1.0 / (total_docs * row_sum)
        row_weight = rescale * row_scale
    column_potential = jnp.log(total_docs * col_scale)
    row_potential = jnp.log(row_scale * row_total)
    assignment = (numerators * (total_docs * row_weight)[:, None] * col_scale[None, :]).astype(
        jnp.bfloat16
    )
    summed = lax.psum_scatter(
        lax.dot_general(
            assignment, embeddings, (((0,), (0,)), ((), ())), preferred_element_type=jnp.float32
        ),
        "docs",
        scatter_dimension=0,
        tiled=True,
    )
    new_prototypes = (
        summed * lax.rsqrt(jnp.mean(summed * summed, axis=1, keepdims=True) + 1e-06)
    ).astype(jnp.bfloat16)
    return (new_prototypes, column_potential, row_potential)


def solution(mesh):
    placed = (P("docs", None), P("protos", None))
    return jax.shard_map(
        on_device,
        mesh=mesh,
        in_specs=placed,
        out_specs=(P(("protos", "docs"), None), P("protos"), P("docs")),
        check_vma=False,
    )
```

profile of v0, /device:TPU:0, one launch (start us, length us, event | category | flops | bytes accessed | tf_op | source)
XLA Modules:
  0.0 816.3 jit_solution(17064669797004932549)
XLA Ops:
  7.2 0.0 copy-start
  7.2 0.0 all-reduce.3.cloned.1.call-start
  7.2 1.2 copy-done
  8.4 31.5 %multiply_reduce_fusion = (f32[1024]{0:T(1024)S(1)}, f32[1024,16384]{1,0:T(8,128)}) fusion(bf16[1024,512]{1,0:T(8,128)(2,1)S(1)} %copy-done, bf16[16384,512]{1,0:T(8,128)(2,1)} %param.3), kind=kOutput, calls=%fused_computation.2 | convolution fusion | flops 17213423616 | bytes 84938752 | tf_op jit(solution)/shard_map/dot_general | solution.py:17
  39.9 11.3 %pmax.7 = f32[1024]{0:T(1024)S(1)} all-reduce(f32[1024]{0:T(1024)S(1)} %get-tuple-element.7), channel_id=1, replica_groups=mesh['docs'=8,'protos'=4] {'protos'}, use_global_device_ids=true, to_apply=%region_1.0 | all-reduce | flops 1024 | bytes 8192 | tf_op jit(solution)/shard_map/pmax | solution.py:22
  51.2 21.2 %fusion.7 = f32[1024]{0:T(1024)S(1)} fusion(f32[1024]{0:T(1024)S(1)} %pmax.7, f32[1024,16384]{1,0:T(8,128)} %get-tuple-element.8), kind=kLoop, calls=%fused_computation.21 | loop fusion | flops 50330624 | bytes 67117056 | tf_op jit(solution)/shard_map/reduce_sum | solution.py:24
  72.4 8.3 %psum.35 = f32[1024]{0:T(1024)S(1)} all-reduce(f32[1024]{0:T(1024)S(1)} %fusion.7), channel_id=1, replica_groups=mesh['docs'=8,'protos'=4] {'protos'}, use_global_device_ids=true, to_apply=%region_3.0 | all-reduce | flops 1024 | bytes 8192 | tf_op jit(solution)/shard_map/psum | solution.py:24
  80.7 46.4 %fusion.6 = f32[1,16384]{1,0:T(1,128)} fusion(f32[1024,1]{0,1:T(1,128)S(1)} %bitcast.20, f32[1024,16384]{1,0:T(8,128)} %get-tuple-element.8, f32[1024]{0:T(1024)S(1)} %pmax.7), kind=kOutput, calls=%fused_computation.20 | convolution fusion | flops 234881024 | bytes 67182592 | tf_op jit(solution)/shard_map/dot_general | solution.py:30
  127.1 0.0 all-reduce.3.cloned.1.call-update
  127.1 0.6 all-reduce.5.cloned.1.call-start
  127.8 53.4 %all-reduce.3.cloned.1.call-done = f32[16384]{0:T(1024)} async-done(((f32[16384]{0:T(1024)}), f32[16384]{0:T(1024)}) %all-reduce.3.cloned.1.call-update) | async-done | bytes 65552 | tf_op jit(solution)/shard_map/psum | solution.py:36
  181.2 0.9 multiply_divide_fusion.1
  182.1 69.4 %fusion.5 = f32[1,1024]{1,0:T(1,128)S(1)} fusion(f32[16384,1]{0,1:T(1,128)S(1)} %bitcast.16, f32[1024,16384]{1,0:T(8,128)} %get-tuple-element.8, f32[1024]{0:T(1024)S(1)} %pmax.7), kind=kOutput, calls=%fused_computation.19 | convolution fusion | flops 234881024 | bytes 67182592 | tf_op jit(solution)/shard_map/dot_general | solution.py:38
  251.5 10.0 %psum.37 = f32[1024]{0:T(1024)S(1)} all-reduce(f32[1024]{0:T(1024)S(1)} %bitcast.21), channel_id=1, replica_groups=mesh['docs'=8,'protos'=4] {'protos'}, use_global_device_ids=true, to_apply=%region_5.0 | all-reduce | flops 1024 | bytes 8192 | tf_op jit(solution)/shard_map/psum | solution.py:44
  261.5 46.4 %fusion.4 = f32[1,16384]{1,0:T(1,128)} fusion(f32[1024,1]{0,1:T(1,128)S(1)} %bitcast.19, f32[1024,16384]{1,0:T(8,128)} %get-tuple-element.8, f32[1024]{0:T(1024)S(1)} %pmax.7), kind=kOutput, calls=%fused_computation.18 | convolution fusion | flops 234881024 | bytes 67182592 | tf_op jit(solution)/shard_map/dot_general | solution.py:30
  307.9 0.0 all-reduce.5.cloned.1.call-update
  307.9 0.3 reduce-scatter.2.cloned.1.call-start
  308.1 50.7 %all-reduce.5.cloned.1.call-done = f32[16384]{0:T(1024)} async-done(((f32[16384]{0:T(1024)}), f32[16384]{0:T(1024)}) %all-reduce.5.cloned.1.call-update) | async-done | bytes 65552 | tf_op jit(solution)/shard_map/psum | solution.py:36
  358.8 1.5 multiply_log_fusion
  360.3 69.4 %fusion.3 = f32[1,1024]{1,0:T(1,128)S(1)} fusion(f32[16384,1]{0,1:T(1,128)S(1)} %bitcast.15, f32[1024,16384]{1,0:T(8,128)} %get-tuple-element.8, f32[1024]{0:T(1024)S(1)} %pmax.7), kind=kOutput, calls=%fused_computation.17 | convolution fusion | flops 234881024 | bytes 67182592 | tf_op jit(solution)/shard_map/dot_general | solution.py:38
  429.7 10.1 %psum.39 = f32[1024]{0:T(1024)S(1)} all-reduce(f32[1024]{0:T(1024)S(1)} %bitcast.22), channel_id=1, replica_groups=mesh['docs'=8,'protos'=4] {'protos'}, use_global_device_ids=true, to_apply=%region_7.0 | all-reduce | flops 1024 | bytes 8192 | tf_op jit(solution)/shard_map/psum | solution.py:44
  439.8 0.6 multiply_log_fusion.1
  440.4 39.8 %fusion = f32[16384,512]{1,0:T(8,128)} fusion(bf16[1024,512]{1,0:T(8,128)(2,1)S(1)} %copy-done, f32[16384]{0:T(1024)S(1)} %get-tuple-element.4, f32[1024]{0:T(1024)S(1)} %get-tuple-element.6, f32[1024,16384]{1,0:T(8,128)} %get-tuple-element.8, f32[1024]{0:T(1024)S(1)} %pmax.7), kind=kOutput, calls=%fused_computation.3 | convolution fusion | flops 17263755264 | bytes 101785600 | tf_op jit(solution)/shard_map/dot_general | solution.py:53
  480.2 0.0 reduce-scatter.2.cloned.1.call-update
  480.2 322.9 %reduce-scatter.2.cloned.1.call-done = f32[2048,512]{1,0:T(8,128)} async-done(((f32[16384,512]{1,0:T(8,128)}), f32[2048,512]{1,0:T(8,128)}) %reduce-scatter.2.cloned.1.call-update) | async-done | bytes 4194320 | tf_op jit(solution)/shard_map/reduce_scatter | solution.py:52
  803.1 2.5 multiply_reduce_fusion.1
  805.7 3.8 multiply_convert_fusion.2
  (3 shorter events, 0.0 us)
Async XLA Ops:
  7.2 1.2 copy-start
  7.2 174.0 %all-reduce.3.cloned.1.call-start = ((), (), s32[]{:S(2)}) async-start(), calls=%async_computation.1 | async-start | bytes 131072 | tf_op jit(solution)/shard_map/psum | solution.py:36
  127.1 231.7 %all-reduce.5.cloned.1.call-start = ((), (), s32[]{:S(2)}) async-start(), calls=%async_computation.2 | async-start | bytes 131072 | tf_op jit(solution)/shard_map/psum | solution.py:36
  307.9 495.2 %reduce-scatter.2.cloned.1.call-start = ((), (), s32[]{:S(2)}) async-start(), calls=%async_computation.3 | async-start | bytes 37748736 | tf_op jit(solution)/shard_map/reduce_scatter | solution.py:52
Sparse Core Ops, SparseCore 0:
  127.3 53.9 all-reduce.2
  308.0 50.7 all-reduce.4
  480.4 322.6 reduce-scatter.1
where the time goes:
time: 820 us; the launch traced here: 816 us
  waiting for transfers between devices  427 us (52%)
  matrix products  303 us (37%)
  blocking collectives  39.7 us (5%)
  other arithmetic  30.6 us (4%)
  between operations  14.1 us (2%)
    reduce_scatter x1, waiting for transfers between devices, on_device(): lax.psum_scatter(lax.dot_general(assignment, embeddings, (((0,), (0,)), (...  323 us
    dot_general x2, matrix products, on_device(): jnp.dot(numerators, col_scale, precision=lax.Precision.HIGHEST, preferred...  139 us
    psum x2, waiting for transfers between devices, on_device(): col_total = lax.psum(col_local, 'docs')  104 us
    dot_general x2, matrix products, on_device(): jnp.dot(row_weight, numerators, precision=lax.Precision.HIGHEST, preferre...  92.8 us
    dot_general x1, matrix products, on_device(): lax.dot_general(assignment, embeddings, (((0,), (0,)), ((), ())), preferr...  39.8 us
    dot_general x1, matrix products, on_device(): lax.dot_general(embeddings, prototypes, (((1,), (1,)), ((), ())), preferr...  31.5 us
    reduce_sum x1, other arithmetic, on_device(): row_total = lax.psum(jnp.sum(numerators, axis=1), 'protos')  21.2 us
    psum x2, blocking collectives, on_device(): row_sum = lax.psum(row_local, 'protos')  20.1 us
  transfers between devices with their start and end apart: 3, of which 3 were waited for; matrix products, arithmetic and copies ran while one was open for 0% of the time, Pallas kernels for 0%

commit v1 on v0

--- a/solution.py
+++ b/solution.py
@@ -33,7 +33,7 @@
             precision=lax.Precision.HIGHEST,
             preferred_element_type=jnp.float32,
         )
-        col_total = lax.psum(col_local, "docs")
+        col_total = jnp.sum(lax.all_gather(col_local, "docs"), axis=0)
         col_scale = 1.0 / (total_protos * col_total)
         row_local = rescale * jnp.dot(
             numerators,

time: 820 us -> 745 us (0.909)
  waiting for transfers between devices: 427 us -> 326 us
  blocking collectives: 39.7 us -> 68.1 us
    psum x2 -> x0, waiting for transfers between devices: 104 us -> none  [on_device(): col_total = lax.psum(col_local, 'docs')]
    all_gather x0 -> x2, blocking collectives: none -> 30.9 us  [on_device(): col_total = jnp.sum(lax.all_gather(col_local, 'docs'), axis=0)]
  transfers between devices with their start and end apart: 3 -> 1, of which waited for: 3 -> 1; matrix products, arithmetic and copies ran while one was open for 0% -> 0% of each run, Pallas kernels for 0% -> 0%
where the time goes in v1:
time: 745 us; the launch traced here: 741 us
  waiting for transfers between devices  326 us (44%)
  matrix products  302 us (41%)
  blocking collectives  68.1 us (9%)
  other arithmetic  29.2 us (4%)
  between operations  14.6 us (2%)
    reduce_scatter x1, waiting for transfers between devices, on_device(): lax.psum_scatter(lax.dot_general(assignment, embeddings, (((0,), (0,)), (...  326 us
    dot_general x2, matrix products, on_device(): jnp.dot(numerators, col_scale, precision=lax.Precision.HIGHEST, preferred...  139 us
    dot_general x2, matrix products, on_device(): jnp.dot(row_weight, numerators, precision=lax.Precision.HIGHEST, preferre...  91.5 us
    dot_general x1, matrix products, on_device(): lax.dot_general(assignment, embeddings, (((0,), (0,)), ((), ())), preferr...  39.8 us
    dot_general x1, matrix products, on_device(): lax.dot_general(embeddings, prototypes, (((1,), (1,)), ((), ())), preferr...  31.5 us
    all_gather x2, blocking collectives, on_device(): col_total = jnp.sum(lax.all_gather(col_local, 'docs'), axis=0)  30.9 us
    reduce_sum x1, other arithmetic, on_device(): row_total = lax.psum(jnp.sum(numerators, axis=1), 'protos')  21.2 us
    psum x2, blocking collectives, on_device(): row_sum = lax.psum(row_local, 'protos')  17.4 us
  transfers between devices with their start and end apart: 1, of which 1 were waited for; matrix products, arithmetic and copies ran while one was open for 0% of the time, Pallas kernels for 0%

profile of v1, /device:TPU:0, one launch (start us, length us, event | category | flops | bytes accessed | tf_op | source)
XLA Modules:
  0.0 741.1 jit_solution(15374560166229347792)
XLA Ops:
  7.2 0.0 copy-start
  7.2 0.0 reduce-scatter.2.cloned.1.call-start
  7.2 1.2 copy-done
  8.4 31.5 %multiply_reduce_fusion = (f32[1024]{0:T(1024)S(1)}, f32[1024,16384]{1,0:T(8,128)}) fusion(bf16[1024,512]{1,0:T(8,128)(2,1)S(1)} %copy-done, bf16[16384,512]{1,0:T(8,128)(2,1)} %param.3), kind=kOutput, calls=%fused_computation.2 | convolution fusion | flops 17213423616 | bytes 84938752 | tf_op jit(solution)/shard_map/dot_general | solution.py:17
  39.9 11.3 %pmax.7 = f32[1024]{0:T(1024)S(1)} all-reduce(f32[1024]{0:T(1024)S(1)} %get-tuple-element.7), channel_id=1, replica_groups=mesh['docs'=8,'protos'=4] {'protos'}, use_global_device_ids=true, to_apply=%region_1.0 | all-reduce | flops 1024 | bytes 8192 | tf_op jit(solution)/shard_map/pmax | solution.py:22
  51.2 21.2 %fusion.7 = f32[1024]{0:T(1024)S(1)} fusion(f32[1024]{0:T(1024)S(1)} %pmax.7, f32[1024,16384]{1,0:T(8,128)} %get-tuple-element.8), kind=kLoop, calls=%fused_computation.21 | loop fusion | flops 50330624 | bytes 67117056 | tf_op jit(solution)/shard_map/reduce_sum | solution.py:24
  72.4 8.5 %psum.21 = f32[1024]{0:T(1024)S(1)} all-reduce(f32[1024]{0:T(1024)S(1)} %fusion.7), channel_id=1, replica_groups=mesh['docs'=8,'protos'=4] {'protos'}, use_global_device_ids=true, to_apply=%region_3.0 | all-reduce | flops 1024 | bytes 8192 | tf_op jit(solution)/shard_map/psum | solution.py:24
  80.9 45.8 %fusion.6 = f32[1,16384]{1,0:T(1,128)S(1)} fusion(f32[1024,1]{0,1:T(1,128)S(1)} %bitcast.20, f32[1024,16384]{1,0:T(8,128)} %get-tuple-element.8, f32[1024]{0:T(1024)S(1)} %pmax.7), kind=kOutput, calls=%fused_computation.20 | convolution fusion | flops 234881024 | bytes 67182592 | tf_op jit(solution)/shard_map/dot_general | solution.py:30
  126.7 15.6 %all-gather = f32[131072]{0:T(1024)S(1)} all-gather(f32[16384]{0:T(1024)S(1)} %bitcast.17), channel_id=2, replica_groups=mesh['docs'=8,'protos'=4] {'docs'}, dimensions={0}, use_global_device_ids=true | all-gather | bytes 589824 | tf_op jit(solution)/shard_map/all_gather | solution.py:36
  142.3 0.1 reshape.20
  142.4 0.1 reduce_sum.37
  142.5 69.4 %fusion.5 = f32[1,1024]{1,0:T(1,128)S(1)} fusion(f32[16384,1]{0,1:T(1,128)S(1)} %bitcast.16, f32[1024,16384]{1,0:T(8,128)} %get-tuple-element.8, f32[1024]{0:T(1024)S(1)} %pmax.7), kind=kOutput, calls=%fused_computation.19 | convolution fusion | flops 234881024 | bytes 67182592 | tf_op jit(solution)/shard_map/dot_general | solution.py:38
  211.9 9.2 %psum.22 = f32[1024]{0:T(1024)S(1)} all-reduce(f32[1024]{0:T(1024)S(1)} %bitcast.21), channel_id=1, replica_groups=mesh['docs'=8,'protos'=4] {'protos'}, use_global_device_ids=true, to_apply=%region_5.0 | all-reduce | flops 1024 | bytes 8192 | tf_op jit(solution)/shard_map/psum | solution.py:44
  221.1 45.8 %fusion.4 = f32[1,16384]{1,0:T(1,128)S(1)} fusion(f32[1024,1]{0,1:T(1,128)S(1)} %bitcast.19, f32[1024,16384]{1,0:T(8,128)} %get-tuple-element.8, f32[1024]{0:T(1024)S(1)} %pmax.7), kind=kOutput, calls=%fused_computation.18 | convolution fusion | flops 234881024 | bytes 67182592 | tf_op jit(solution)/shard_map/dot_general | solution.py:30
  266.9 15.3 %all-gather.1 = f32[131072]{0:T(1024)S(1)} all-gather(f32[16384]{0:T(1024)S(1)} %bitcast.18), channel_id=3, replica_groups=mesh['docs'=8,'protos'=4] {'docs'}, dimensions={0}, use_global_device_ids=true | all-gather | bytes 589824 | tf_op jit(solution)/shard_map/all_gather | solution.py:36
  282.1 0.1 reshape.21
  282.2 0.1 reduce_sum.38
  282.4 0.7 multiply_log_fusion
  283.0 69.4 %fusion.3 = f32[1,1024]{1,0:T(1,128)S(1)} fusion(f32[16384,1]{0,1:T(1,128)S(1)} %bitcast.15, f32[1024,16384]{1,0:T(8,128)} %get-tuple-element.8, f32[1024]{0:T(1024)S(1)} %pmax.7), kind=kOutput, calls=%fused_computation.17 | convolution fusion | flops 234881024 | bytes 67182592 | tf_op jit(solution)/shard_map/dot_general | solution.py:38
  352.4 8.3 %psum.23 = f32[1024]{0:T(1024)S(1)} all-reduce(f32[1024]{0:T(1024)S(1)} %bitcast.22), channel_id=1, replica_groups=mesh['docs'=8,'protos'=4] {'protos'}, use_global_device_ids=true, to_apply=%region_7.0 | all-reduce | flops 1024 | bytes 8192 | tf_op jit(solution)/shard_map/psum | solution.py:44
  360.7 0.6 multiply_log_fusion.1
  361.3 39.8 %fusion = f32[16384,512]{1,0:T(8,128)} fusion(bf16[1024,512]{1,0:T(8,128)(2,1)S(1)} %copy-done, f32[16384]{0:T(1024)S(1)} %get-tuple-element.4, f32[1024]{0:T(1024)S(1)} %get-tuple-element.6, f32[1024,16384]{1,0:T(8,128)} %get-tuple-element.8, f32[1024]{0:T(1024)S(1)} %pmax.7), kind=kOutput, calls=%fused_computation.3 | convolution fusion | flops 17263755264 | bytes 101785600 | tf_op jit(solution)/shard_map/dot_general | solution.py:53
  401.1 0.0 reduce-scatter.2.cloned.1.call-update
  401.1 326.3 %reduce-scatter.2.cloned.1.call-done = f32[2048,512]{1,0:T(8,128)} async-done(((f32[16384,512]{1,0:T(8,128)}), f32[2048,512]{1,0:T(8,128)}) %reduce-scatter.2.cloned.1.call-update) | async-done | bytes 4194320 | tf_op jit(solution)/shard_map/reduce_scatter | solution.py:52
  727.4 2.5 multiply_reduce_fusion.1
  729.9 3.8 multiply_convert_fusion.2
  (4 shorter events, 0.0 us)
Async XLA Ops:
  7.2 1.2 copy-start
  7.2 720.2 %reduce-scatter.2.cloned.1.call-start = ((), (), s32[]{:S(2)}) async-start(), calls=%async_computation.1 | async-start | bytes 37748736 | tf_op jit(solution)/shard_map/reduce_scatter | solution.py:52
Sparse Core Ops, SparseCore 0:
  401.2 326.1 reduce-scatter.1
